TPU v7x, 256 devices: a whole 4x4x8 slice. The times are simulated.
256 devices in a mesh: seq: 32 (over z_hi, y, core), pair: 8 (over z_lo, x).
Axes of the slice: x: 4, y: 4, z: 8 (z_hi: 4, z_lo: 2; z = z_hi * 2 + z_lo), core: 2. Of those that a mesh axis runs over, the one named last changes fastest.
Arguments:
- student: float32 [20480, 1408], P('seq'), may hold values from -640 to 640
- teacher: float32 [20480, 1408], P('seq'), may hold values from -640 to 640
Outputs:
- student_grad: float32 [20480, 1408], P('seq')
All inputs are finite; a program needn't handle non-finite values.
Results may differ from a plain program's by a relative error of at most 0.0059.
Values may be sent and summed in bfloat16 or wider, within the bound.
A program may use at most 64 MiB of HBM per device.

v0:
```python
import math

import jax
import jax.numpy as jnp
from jax import lax
from jax.sharding import PartitionSpec as P


def from_behind(block, axis, distance):
    devices = range(lax.axis_size(axis))
    route = [((i - distance) % len(devices), i) for i in devices]
    return lax.ppermute(block, axis, route)


def normalize(values, width):
    scale = lax.rsqrt(jnp.sum(values * values, axis=1, keepdims=True) + width * 1e-06)
    return (scale, values * scale)


def relation_tile(own_s, own_t, partner, margin, weight):
    contract = (((1,), (1,)), ((), ()))
    s_rel = lax.dot_general(own_s, partner[0], contract, preferred_element_type=jnp.float32)
    t_rel = lax.dot_general(own_t, partner[1], contract, preferred_element_type=jnp.float32)
    delta = s_rel - t_rel
    shrink = jnp.maximum(delta - margin, 0.0) + jnp.minimum(delta + margin, 0.0)
    relation = (weight * shrink).astype(jnp.bfloat16)
    return jnp.dot(relation, partner[0], preferred_element_type=jnp.float32)


def finish_rows(scale, unit, unit_grad):
    dotted = jnp.sum(unit * unit_grad, axis=1, keepdims=True)
    return scale * (unit_grad - unit * dotted)


def local(student, teacher):
    rows, width = student.shape
    seq_count = lax.axis_size("seq")
    pair_count = lax.axis_size("pair")
    block_count = seq_count // pair_count
    bit_count = pair_count.bit_length() - 1
    pair_index = lax.axis_index("pair")
    margin = 0.75 / math.sqrt(width)
    weight = 64.0 * width / math.sqrt(rows * seq_count)
    s_scale, s_unit = normalize(student, width)
    t_scale, t_unit = normalize(teacher, width)
    s_half = s_unit.astype(jnp.bfloat16)
    t_half = t_unit.astype(jnp.bfloat16)
    partner = jnp.stack([s_half, t_half])

    def tile(block):
        return relation_tile(s_half, t_half, block, margin, weight)

    for bit in range(bit_count):
        moved = from_behind(partner, "seq", 1 << bit)
        partner = jnp.where(pair_index // (1 << bit) % 2 == 1, moved, partner)

    def advance(step, carry):
        block, total = carry
        block = from_behind(block, "seq", pair_count)
        return (block, total + tile(block))

    partial_value = tile(partner)
    partner, partial_value = lax.fori_loop(0, block_count - 1, advance, (partner, partial_value))
    unit_grad = lax.psum(partial_value, "pair")
    return finish_rows(s_scale, s_unit, unit_grad)


def solution(mesh):
    placed = (P("seq", None), P("seq", None))
    return jax.shard_map(
        local, mesh=mesh, in_specs=placed, out_specs=P("seq", None), check_vma=False
    )
```

profile of v0, /device:TPU:2, one launch (start us, length us, event | category | flops | bytes accessed | tf_op | source)
XLA Modules:
  0.0 1076.2 jit_solution(164027926578918337)
XLA Ops:
  6.5 0.0 all-reduce.2.cloned.1.call-start
  6.5 0.0 copy-start
  6.5 0.0 copy-start.3
  6.5 2.5 multiply_reduce_fusion.1
  9.0 0.6 copy-done
  9.6 0.3 multiply_reduce_fusion.2
  10.0 0.8 copy-done.3
  10.7 0.5 multiply_convert_fusion.1
  11.2 0.0 copy-start.2
  11.2 2.4 pad_maximum_fusion
  13.6 0.0 copy-done.2
  13.6 0.0 collective-permute-start.1
  13.6 63.7 %collective-permute-done.1 = bf16[2,640,1408]{2,1,0:T(8,128)(2,1)} collective-permute-done((bf16[2,640,1408]{2,1,0:T(8,128)(2,1)}, bf16[2,640,1408]{2,1,0:T(8,128)(2,1)}, u32[]{:S(2)}, u32[]{:S(2)}) %collective-permute-start.1) | collective-permute-done | bytes 3604512 | tf_op jit(solution)/shard_map/ppermute | solution.py:12
  77.4 4.9 broadcast_select_fusion
  82.2 0.0 collective-permute-start.2
  82.2 158.5 %collective-permute-done.2 = bf16[2,640,1408]{2,1,0:T(8,128)(2,1)} collective-permute-done((bf16[2,640,1408]{2,1,0:T(8,128)(2,1)}, bf16[2,640,1408]{2,1,0:T(8,128)(2,1)}, u32[]{:S(2)}, u32[]{:S(2)}) %collective-permute-start.2) | collective-permute-done | bytes 3604512 | tf_op jit(solution)/shard_map/ppermute | solution.py:12
  240.7 4.0 broadcast_select_fusion.1
  244.8 0.0 collective-permute-start.3
  244.8 236.8 %collective-permute-done.3 = bf16[2,640,1408]{2,1,0:T(8,128)(2,1)} collective-permute-done((bf16[2,640,1408]{2,1,0:T(8,128)(2,1)}, bf16[2,640,1408]{2,1,0:T(8,128)(2,1)}, u32[]{:S(2)}, u32[]{:S(2)}) %collective-permute-start.3) | collective-permute-done | bytes 3604512 | tf_op jit(solution)/shard_map/ppermute | solution.py:12
  481.6 2.4 broadcast_select_fusion.2
  484.0 0.0 copy-start.5
  484.0 1.8 copy-done.5
  485.8 1.7 fusion.10
  487.5 8.1 fusion.11
  495.6 462.4 %while.14 = (s32[]{:T(128)}, bf16[2,640,1408]{2,1,0:T(8,128)(2,1)}, f32[640,1408]{1,0:T(8,128)}, bf16[640,1408]{1,0:T(8,128)(2,1)}, bf16[640,1408]{1,0:T(8,128)(2,1)S(1)}, /*index=5*/s32[]{:T(128)}) while((s32[]{:T(128)}, bf16[2,640,1408]{2,1,0:T(8,128)(2,1)}, f32[640,1408]{1,0:T(8,128)}, bf16[640,1408]{1,0:T(8,128)(2,1)}, ...), condition=%wide.region_3.4_spmd, body=%wide.region_2.3_spmd.sunk | while | flops 3464478720 | bytes 41123948 | solution.py:63
  495.6 0.0 collective-permute-start
  495.6 156.2 %collective-permute-done = bf16[2,640,1408]{2,1,0:T(8,128)(2,1)} collective-permute-done((bf16[2,640,1408]{2,1,0:T(8,128)(2,1)}, bf16[2,640,1408]{2,1,0:T(8,128)(2,1)}, u32[]{:S(2)}, u32[]{:S(2)}) %collective-permute-start) | collective-permute-done | bytes 3604512 | tf_op jit(solution)/shard_map/while/body/eval_jaxpr/ppermute | solution.py:12
  651.8 4.1 copy.10
  655.9 3.2 fusion.30
  659.1 9.1 convolution_add_fusion.2
  668.3 94.3 %collective-permute-start = (bf16[2,640,1408]{2,1,0:T(8,128)(2,1)}, bf16[2,640,1408]{2,1,0:T(8,128)(2,1)}, u32[]{:S(2)}, u32[]{:S(2)}) collective-permute-start(bf16[2,640,1408]{2,1,0:T(8,128)(2,1)} %get-tuple-element.121), channel_id=1, source_target_pairs={{192,0},{200,8},{208,16},{216,24},{224,32},{232,40},{240,48},{248,... | collective-permute-start | bytes 10813448 | tf_op jit(solution)/shard_map/while/body/eval_jaxpr/ppermute | solution.py:12
  762.6 80.8 %collective-permute-done = bf16[2,640,1408]{2,1,0:T(8,128)(2,1)} collective-permute-done((bf16[2,640,1408]{2,1,0:T(8,128)(2,1)}, bf16[2,640,1408]{2,1,0:T(8,128)(2,1)}, u32[]{:S(2)}, u32[]{:S(2)}) %collective-permute-start) | collective-permute-done | bytes 3604512 | tf_op jit(solution)/shard_map/while/body/eval_jaxpr/ppermute | solution.py:12
  843.4 4.1 copy.10
  847.5 3.2 fusion.30
  850.7 9.1 convolution_add_fusion.2
  859.8 1.5 collective-permute-start
  861.3 80.3 %collective-permute-done = bf16[2,640,1408]{2,1,0:T(8,128)(2,1)} collective-permute-done((bf16[2,640,1408]{2,1,0:T(8,128)(2,1)}, bf16[2,640,1408]{2,1,0:T(8,128)(2,1)}, u32[]{:S(2)}, u32[]{:S(2)}) %collective-permute-start) | collective-permute-done | bytes 3604512 | tf_op jit(solution)/shard_map/while/body/eval_jaxpr/ppermute | solution.py:12
  941.6 4.1 copy.10
  945.7 3.2 fusion.30
  948.9 9.1 convolution_add_fusion.2
  958.0 0.0 all-reduce.2.cloned.1.call-update
  958.1 103.7 %all-reduce.2.cloned.1.call-done = f32[640,1408]{1,0:T(8,128)} async-done(((f32[640,1408]{1,0:T(8,128)}), f32[640,1408]{1,0:T(8,128)}) %all-reduce.2.cloned.1.call-update) | async-done | bytes 3604496 | tf_op jit(solution)/shard_map/psum | solution.py:64
  1061.8 0.0 copy-start.1
  1061.8 0.0 copy-start.4
  1061.8 3.7 multiply_reduce_fusion
  1065.5 0.4 copy-done.1
  1065.9 1.1 copy-done.4
  1067.0 2.4 subtract_multiply_fusion
  (2 shorter events, 0.0 us)
Async XLA Ops:
  6.5 1055.2 %all-reduce.2.cloned.1.call-start = ((), (), s32[]{:S(2)}) async-start(), calls=%async_computation | async-start | bytes 7208960 | tf_op jit(solution)/shard_map/psum | solution.py:64
  6.5 3.1 copy-start
  6.5 4.2 copy-start.3
  11.2 2.4 copy-start.2
  13.6 63.7 %collective-permute-start.1 = (bf16[2,640,1408]{2,1,0:T(8,128)(2,1)}, bf16[2,640,1408]{2,1,0:T(8,128)(2,1)}, u32[]{:S(2)}, u32[]{:S(2)}) collective-permute-start(bf16[2,640,1408]{2,1,0:T(8,128)(2,1)} %pad_maximum_fusion), channel_id=1, source_target_pairs={{248,0},{0,8},{8,16},{16,24},{24,32},{32,40},{40,48},{48,56},{56,6... | collective-permute-start | bytes 10813448 | tf_op jit(solution)/shard_map/ppermute | solution.py:12
  82.2 158.5 %collective-permute-start.2 = (bf16[2,640,1408]{2,1,0:T(8,128)(2,1)}, bf16[2,640,1408]{2,1,0:T(8,128)(2,1)}, u32[]{:S(2)}, u32[]{:S(2)}) collective-permute-start(bf16[2,640,1408]{2,1,0:T(8,128)(2,1)} %broadcast_select_fusion), channel_id=1, source_target_pairs={{240,0},{248,8},{0,16},{8,24},{16,32},{24,40},{32,48},{40,56},{48,... | collective-permute-start | bytes 10813448 | tf_op jit(solution)/shard_map/ppermute | solution.py:12
  244.8 236.8 %collective-permute-start.3 = (bf16[2,640,1408]{2,1,0:T(8,128)(2,1)}, bf16[2,640,1408]{2,1,0:T(8,128)(2,1)}, u32[]{:S(2)}, u32[]{:S(2)}) collective-permute-start(bf16[2,640,1408]{2,1,0:T(8,128)(2,1)} %broadcast_select_fusion.1), channel_id=1, source_target_pairs={{224,0},{232,8},{240,16},{248,24},{0,32},{8,40},{16,48},{24,56},{3... | collective-permute-start | bytes 10813448 | tf_op jit(solution)/shard_map/ppermute | solution.py:12
  484.0 1.8 copy-start.5
  495.6 156.2 %collective-permute-start = (bf16[2,640,1408]{2,1,0:T(8,128)(2,1)}, bf16[2,640,1408]{2,1,0:T(8,128)(2,1)}, u32[]{:S(2)}, u32[]{:S(2)}) collective-permute-start(bf16[2,640,1408]{2,1,0:T(8,128)(2,1)} %get-tuple-element.121), channel_id=1, source_target_pairs={{192,0},{200,8},{208,16},{216,24},{224,32},{232,40},{240,48},{248,... | collective-permute-start | bytes 10813448 | tf_op jit(solution)/shard_map/while/body/eval_jaxpr/ppermute | solution.py:12
  668.3 175.1 %collective-permute-start = (bf16[2,640,1408]{2,1,0:T(8,128)(2,1)}, bf16[2,640,1408]{2,1,0:T(8,128)(2,1)}, u32[]{:S(2)}, u32[]{:S(2)}) collective-permute-start(bf16[2,640,1408]{2,1,0:T(8,128)(2,1)} %get-tuple-element.121), channel_id=1, source_target_pairs={{192,0},{200,8},{208,16},{216,24},{224,32},{232,40},{240,48},{248,... | collective-permute-start | bytes 10813448 | tf_op jit(solution)/shard_map/while/body/eval_jaxpr/ppermute | solution.py:12
  859.8 81.8 %collective-permute-start = (bf16[2,640,1408]{2,1,0:T(8,128)(2,1)}, bf16[2,640,1408]{2,1,0:T(8,128)(2,1)}, u32[]{:S(2)}, u32[]{:S(2)}) collective-permute-start(bf16[2,640,1408]{2,1,0:T(8,128)(2,1)} %get-tuple-element.121), channel_id=1, source_target_pairs={{192,0},{200,8},{208,16},{216,24},{224,32},{232,40},{240,48},{248,... | collective-permute-start | bytes 10813448 | tf_op jit(solution)/shard_map/while/body/eval_jaxpr/ppermute | solution.py:12
  1061.8 4.1 copy-start.1
  1061.8 5.2 copy-start.4
Sparse Core Ops, SparseCore 0:
  958.2 103.5 all-reduce.1
where the time goes:
time: 1080 us
  waiting for transfers between devices  880 us (81%)
  starting transfers between devices  95.9 us (9%)
  matrix products  46.7 us (4%)
  other arithmetic  23.1 us (2%)
  local copies, waits for them, and re-layouts  17 us (2%)
  between operations  13.4 us (1%)
    ppermute x6, waiting for transfers between devices, from_behind(): return lax.ppermute(block, axis, route)  776 us
    psum x1, waiting for transfers between devices, local(): unit_grad = lax.psum(partial_value, 'pair')  104 us
    ppermute x6, starting transfers between devices, from_behind(): return lax.ppermute(block, axis, route)  95.9 us
    dot_general x4, matrix products, relation_tile(): return jnp.dot(relation, partner[0], preferred_element_type=jnp.float32)  35.5 us
  transfers between devices with their start and end apart: 7, of which 7 were waited for; matrix products, arithmetic and copies ran while one was open for 0% of the time, Pallas kernels for 0%

commit v1 on v0

v1 whole, which is shorter than its diff:
```python
import functools
import math

import jax
import jax.numpy as jnp
from jax import lax
from jax.experimental import pallas as pl
from jax.experimental.pallas import tpu as pltpu
from jax.sharding import PartitionSpec as P

MESH = pl.DeviceIdType.MESH
UNIT = 80
GROUP = 256
TILE = 320
PARTS = ((0, 512), (512, 512), (1024, 384))
ORDERS = ((0, 1, 2), (1, 2, 0), (2, 0, 1))

NAMES = (
    ["v", "v2", "w"]
    + [item + way for item in ("a", "v", "p", "w") for way in ("+", "-", "f")]
    + ["k0", "k1", "x0", "x1"]
    + [f"r{part}{step}" for part in range(3) for step in range(3)]
    + [f"g{part}{step}" for part in range(3) for step in range(3)]
)
INDEX = {name: i for i, name in enumerate(NAMES)}


def normalize(values, width):
    scale = lax.rsqrt(jnp.sum(values * values, axis=1, keepdims=True) + width * 1e-06)
    return scale, values * scale


def kernel(
    student, teacher, out,
    quarter_s, quarter_t, full_s, full_t, far, cols, own, total, other,
    rs_send, rs_recv, gathered, acc, load_sem, send_sem, recv_sem,
):
    rows, width = student.shape
    margin = 0.75 / math.sqrt(width)
    weight = 64.0 * width / math.sqrt(rows * lax.axis_size("seq"))

    seq, pair = lax.axis_index("seq"), lax.axis_index("pair")
    core, y, z_hi = seq % 2, (seq // 2) % 4, seq // 8
    z_lo, x = pair // 4, pair % 4
    z = z_hi * 2 + z_lo
    side = 2 * z_lo - 1

    def device(x=x, y=y, z=z, core=core):
        return ((z // 2 * 4 + y) * 2 + core, (z % 2) * 4 + x)

    up, down = device(y=(y + 1) % 4), device(y=(y + 3) % 4)
    near_z = device(z=(z + side + 8) % 8)
    after_z, before_z = device(z=(z - 2 * side + 8) % 8), device(z=(z + 2 * side + 8) % 8)
    sibling = device(core=1 - core)
    cube = (device(x=x + 1 - 2 * (x % 2)), device(x=3 - x), device(z=z + 1 - 2 * z_lo))
    bits = (((x + 1) // 2) % 2, x // 2, z_lo)

    def copy(name, src, dst, target):
        i = INDEX[name]
        return pltpu.make_async_remote_copy(
            src_ref=src, dst_ref=dst, send_sem=send_sem.at[i], recv_sem=recv_sem.at[i],
            device_id=target, device_id_type=MESH,
        )

    started = {}

    def send(name, src, dst, target):
        started[name] = copy(name, src, dst, target)
        started[name].start()

    def arrived(*names):
        for name in names:
            started[name].wait_recv()

    first = pl.multiple_of(x * (2 * UNIT), 2 * UNIT)
    loads = [
        pltpu.make_async_copy(student.at[pl.ds(first, 2 * UNIT)], quarter_s, load_sem.at[0]),
        pltpu.make_async_copy(teacher.at[pl.ds(first, 2 * UNIT)], quarter_t, load_sem.at[1]),
        pltpu.make_async_copy(student, full_s, load_sem.at[2]),
        pltpu.make_async_copy(teacher, full_t, load_sem.at[3]),
    ]
    for load in loads:
        load.start()

    barrier = pltpu.get_barrier_semaphore()
    peers = (up, down, near_z, after_z, before_z, sibling) + cube
    for peer in peers:
        pl.semaphore_signal(barrier, inc=1, device_id=peer, device_id_type=MESH)

    def slot(i):
        return cols.at[pl.ds(i * UNIT, UNIT)]

    (A, A_DOWN, A_UP, V, V_DOWN, V_UP, Q, W, A_FAR, V_FAR,
     Q_DOWN, Q_UP, W_DOWN, W_UP, Q_FAR, W_FAR) = range(16)

    loads[0].wait()
    loads[1].wait()
    mine = pl.multiple_of(z_lo * UNIT, UNIT)
    theirs = pl.multiple_of((1 - z_lo) * UNIT, UNIT)
    far[:, :width] = normalize(quarter_s[pl.ds(theirs, UNIT)], width)[1].astype(jnp.bfloat16)
    far[:, width:] = normalize(quarter_t[pl.ds(theirs, UNIT)], width)[1].astype(jnp.bfloat16)
    cols[:UNIT, :width] = normalize(quarter_s[pl.ds(mine, UNIT)], width)[1].astype(jnp.bfloat16)
    cols[:UNIT, width:] = normalize(quarter_t[pl.ds(mine, UNIT)], width)[1].astype(jnp.bfloat16)
    pl.semaphore_wait(barrier, len(peers))
    send("v", far, slot(V), near_z)
    send("a+", slot(A), slot(A_DOWN), up)
    send("a-", slot(A), slot(A_UP), down)
    send("v2", slot(A), slot(Q), near_z)

    loads[2].wait()
    loads[3].wait()
    for half in range(2):

        @pl.loop(0, TILE // UNIT)
        def _(i):
            at = pl.ds(pl.multiple_of(half * TILE + i * UNIT, UNIT), UNIT)
            own[0, at, :width] = normalize(full_s[at], width)[1].astype(jnp.bfloat16)
            own[0, at, width:] = -(normalize(full_t[at], width)[1].astype(jnp.bfloat16))
            total[0, at] = jnp.zeros((UNIT, width), jnp.float32)
            total[1, at] = jnp.zeros((UNIT, width), jnp.float32)

        at = pl.ds(half * TILE, TILE)
        send(f"k{half}", own.at[0, at], own.at[1, at], sibling)

    def relate(group, block, tile):
        at = pl.ds(tile * TILE, TILE)
        tokens = pl.ds(group * GROUP, GROUP)
        delta = lax.dot_general(
            own[block, at, :], cols[tokens, :], (((1,), (1,)), ((), ())),
            preferred_element_type=jnp.float32,
        )
        shrink = jnp.maximum(delta - margin, 0.0) + jnp.minimum(delta + margin, 0.0)
        relation = (weight * shrink).astype(jnp.bfloat16)
        for start, size in PARTS:
            total[block, at, pl.ds(start, size)] += jnp.dot(
                relation, cols[tokens, pl.ds(start, size)], preferred_element_type=jnp.float32
            )

    def relate_all(group):
        @pl.loop(0, 2)
        def _(block):
            for tile in range(rows // TILE):
                relate(group, block, tile)

    arrived("v", "a+", "a-")
    send("v+", slot(V), slot(V_DOWN), up)
    send("v-", slot(V), slot(V_UP), down)
    send("w", slot(V), slot(W), after_z)
    send("af", slot(A_DOWN), slot(A_FAR), up)
    arrived("k0", "k1")
    relate_all(0)
    arrived("v+", "v-", "v2")
    send("vf", slot(V_UP), slot(V_FAR), down)
    send("p+", slot(Q), slot(Q_DOWN), up)
    send("p-", slot(Q), slot(Q_UP), down)
    relate_all(1)
    arrived("w", "af", "vf")
    send("w+", slot(W), slot(W_DOWN), up)
    send("w-", slot(W), slot(W_UP), down)
    relate_all(2)
    arrived("p+", "p-")
    send("pf", slot(Q_DOWN), slot(Q_FAR), up)
    arrived("w+", "w-")
    send("wf", slot(W_UP), slot(W_FAR), down)
    relate_all(3)
    arrived("pf", "wf")
    for tile in range(2):
        at = pl.ds(tile * TILE, TILE)
        relate(4, 1, tile)
        send(f"x{tile}", total.at[1, at], other.at[at], sibling)
    for tile in range(2):
        relate(4, 0, tile)
    arrived("x0", "x1")

    def chunk(order, *place):
        strides = (4, 2, 1)
        index = sum(strides[d] * i for d, i in zip(order, place))
        return pl.ds(pl.multiple_of(index * UNIT, UNIT), UNIT)

    for part, (start, size) in enumerate(PARTS):
        order, at = ORDERS[part], pl.ds(start, size)
        b = [bits[d] for d in order]
        for i in range(4):
            rows_at = chunk(order, 1 - b[0], i // 2, i % 2)
            rs_send[part][i] = (total[0, rows_at, at] + other[rows_at, at]).astype(jnp.bfloat16)
        send(f"r{part}0", rs_send[part].at[0:4], rs_recv[part].at[0:4], cube[order[0]])
    for part, (start, size) in enumerate(PARTS):
        order, at = ORDERS[part], pl.ds(start, size)
        b = [bits[d] for d in order]
        arrived(f"r{part}0")
        for i in range(2):
            rows_at = chunk(order, b[0], 1 - b[1], i)
            got = rs_recv[part][2 * (1 - b[1]) + i].astype(jnp.float32)
            rs_send[part][4 + i] = (
                total[0, rows_at, at] + other[rows_at, at] + got
            ).astype(jnp.bfloat16)
        send(f"r{part}1", rs_send[part].at[4:6], rs_recv[part].at[4:6], cube[order[1]])
    for part, (start, size) in enumerate(PARTS):
        order, at = ORDERS[part], pl.ds(start, size)
        b = [bits[d] for d in order]
        arrived(f"r{part}1")
        for i, place in enumerate((1 - b[2], b[2])):
            rows_at = chunk(order, b[0], b[1], place)
            value = (
                total[0, rows_at, at] + other[rows_at, at]
                + rs_recv[part][2 * b[1] + place].astype(jnp.float32)
                + rs_recv[part][4 + place].astype(jnp.float32)
            )
            if i == 0:
                rs_send[part][6] = value.astype(jnp.bfloat16)
                send(f"r{part}2", rs_send[part].at[6:7], rs_recv[part].at[6:7], cube[order[2]])
            else:
                acc[:, at] = value
    for part, (start, size) in enumerate(PARTS):
        at = pl.ds(start, size)
        arrived(f"r{part}2")
        acc[:, at] += rs_recv[part][6].astype(jnp.float32)

    rows_at = chunk((0, 1, 2), *bits)
    scale, unit = normalize(full_s[rows_at], width)
    unit_grad = acc[...]
    dotted = jnp.sum(unit * unit_grad, axis=1, keepdims=True)
    grad = (scale * (unit_grad - unit * dotted)).astype(jnp.bfloat16)
    for part, (start, size) in enumerate(PARTS):
        order = ORDERS[part]
        b = [bits[d] for d in order]
        gathered[part][b[0], b[1], b[2]] = grad[:, start:start + size]
        mine_at = gathered[part].at[b[0], b[1], b[2]]
        send(f"g{part}0", mine_at, mine_at, cube[order[2]])
    for part in range(3):
        order = ORDERS[part]
        b = [bits[d] for d in order]
        arrived(f"g{part}0")
        mine_at = gathered[part].at[b[0], b[1]]
        send(f"g{part}1", mine_at, mine_at, cube[order[1]])
    for part in range(3):
        order = ORDERS[part]
        b = [bits[d] for d in order]
        arrived(f"g{part}1")
        mine_at = gathered[part].at[b[0]]
        send(f"g{part}2", mine_at, mine_at, cube[order[0]])
    for part, (start, size) in enumerate(PARTS):
        order = ORDERS[part]
        arrived(f"g{part}2")
        for i in range(8):
            place = (i // 4, i // 2 % 2, i % 2)
            out[i * UNIT:(i + 1) * UNIT, start:start + size] = gathered[part][
                tuple(place[d] for d in order)
            ]
    for name in NAMES:
        started[name].wait_send()


def local(student, teacher):
    rows, width = student.shape
    bf16, f32 = jnp.bfloat16, jnp.float32

    def body(student, teacher, out, *scratch):
        plain, parts = scratch[:9], scratch[9:18]
        kernel(student, teacher, out, *plain, parts[0:3], parts[3:6], parts[6:9], *scratch[18:])

    grad = pl.pallas_call(
        body,
        out_shape=jax.ShapeDtypeStruct((rows, width), bf16),
        in_specs=[pl.BlockSpec(memory_space=pl.ANY)] * 2,
        out_specs=pl.BlockSpec(memory_space=pltpu.VMEM),
        scratch_shapes=[
            pltpu.VMEM((2 * UNIT, width), f32),
            pltpu.VMEM((2 * UNIT, width), f32),
            pltpu.VMEM((rows, width), f32),
            pltpu.VMEM((rows, width), f32),
            pltpu.VMEM((UNIT, 2 * width), bf16),
            pltpu.VMEM((2 * rows, 2 * width), bf16),
            pltpu.VMEM((2, rows, 2 * width), bf16),
            pltpu.VMEM((2, rows, width), f32),
            pltpu.VMEM((rows, width), f32),
        ]
        + [pltpu.VMEM((7, UNIT, size), bf16) for _, size in PARTS] * 2
        + [pltpu.VMEM((2, 2, 2, UNIT, size), bf16) for _, size in PARTS]
        + [
            pltpu.VMEM((UNIT, width), f32),
            pltpu.SemaphoreType.DMA((4,)),
            pltpu.SemaphoreType.DMA((len(NAMES),)),
            pltpu.SemaphoreType.DMA((len(NAMES),)),
        ],
        compiler_params=pltpu.CompilerParams(
            collective_id=0, has_side_effects=True, vmem_limit_bytes=56 << 20
        ),
        name="relation_grad",
    )(student, teacher)
    return grad.astype(f32)


def solution(mesh):
    placed = (P("seq", None), P("seq", None))
    return jax.shard_map(
        local, mesh=mesh, in_specs=placed, out_specs=P("seq", None), check_vma=False
    )
```

time: 1080 us -> 127 us (0.12)
  waiting for transfers between devices: 880 us -> 0 us
  Pallas kernels: 0 us -> 123 us
  starting transfers between devices: 95.9 us -> 0 us
  matrix products: 46.7 us -> 0 us
  other arithmetic: 23.1 us -> 3.56 us
  local copies, waits for them, and re-layouts: 17 us -> 0 us
  between operations: 13.4 us -> 0.01 us
    ppermute x6 -> x0, waiting for transfers between devices: 776 us -> none  [from_behind(): return lax.ppermute(block, axis, route)]
    pallas_call x0 -> x1, Pallas kernels: none -> 123 us  [local(): pl.pallas_call(body, out_shape=jax.ShapeDtypeStruct((rows, width), bf16),...]
    psum x1 -> x0, waiting for transfers between devices: 104 us -> none  [local(): unit_grad = lax.psum(partial_value, 'pair')]
    ppermute x6 -> x0, starting transfers between devices: 95.9 us -> none  [from_behind(): return lax.ppermute(block, axis, route)]
    dot_general x8 -> x0, matrix products: 46.7 us -> none  [the longest x4 35.5 us: relation_tile(): return jnp.dot(relation, partner[0], preferred_element_type=jnp.float32)]
    while x3 -> x0, local copies, waits for them, and re-layouts: 12.3 us -> none
    select_n x3 -> x0, other arithmetic: 11.3 us -> none  [local(): partner = jnp.where(pair_index // (1 << bit) % 2 == 1, moved, partner)]
  transfers between devices with their start and end apart: 7 -> 0, of which waited for: 7 -> 0; matrix products, arithmetic and copies ran while one was open for 0% -> 0% of each run, Pallas kernels for 0% -> 0%
where the time goes in v1:
time: 127 us; the launch traced here: 126 us
  Pallas kernels  123 us (97%)
  other arithmetic  3.56 us (3%)
    pallas_call x1, Pallas kernels, local(): pl.pallas_call(body, out_shape=jax.ShapeDtypeStruct((rows, width), bf16),...  123 us
    convert_element_type x1, other arithmetic, local(): return grad.astype(f32)  3.56 us

profile of v1, /device:TPU:2, one launch (start us, length us, event | category | flops | bytes accessed | tf_op | source)
XLA Modules:
  0.0 126.4 jit_solution(6005089667856691311)
XLA Ops:
  0.0 122.8 %relation_grad.1 = bf16[640,1408]{1,0:T(8,128)(2,1)} custom-call(f32[640,1408]{1,0:T(8,128)} %student.1, f32[640,1408]{1,0:T(8,128)} %teacher.1), custom_call_target="tpu_custom_call" | custom-call | tf_op jit(solution)/shard_map/relation_grad/pallas_call | solution.py:262
  122.8 3.6 %convert_element_type.3 = f32[640,1408]{1,0:T(8,128)} convert(bf16[640,1408]{1,0:T(8,128)(2,1)} %relation_grad.1) | non-fusion elementwise | flops 901120 | bytes 5406720 | tf_op jit(solution)/shard_map/convert_element_type | solution.py:291

commit v2 on v1

v2 whole, which is shorter than its diff:
```python
import functools
import math

import jax
import jax.numpy as jnp
from jax import lax
from jax.experimental import pallas as pl
from jax.experimental.pallas import tpu as pltpu
from jax.sharding import PartitionSpec as P

MESH = pl.DeviceIdType.MESH
UNIT = 80
GROUP = 256
TILE = 320
WAVES = ((0, 48), (48, 32))
PARTS = ((0, 512), (512, 512), (1024, 384))
ORDERS = ((0, 1, 2), (1, 2, 0), (2, 0, 1))

NAMES = (
    ["v", "q", "w", "qd", "qu", "qf"]
    + [item + way for item in ("a", "v", "w") for way in ("+", "-", "f")]
    + ["k0", "k1", "x", "e0", "e1", "e2", "e3"]
    + [f"{kind}{part}{step}{wave}" for kind in "rg"
       for part in range(3) for step in range(3) for wave in range(2)]
)
INDEX = {name: i for i, name in enumerate(NAMES)}


def normalize(values, width):
    scale = lax.rsqrt(jnp.sum(values * values, axis=1, keepdims=True) + width * 1e-06)
    return scale, values * scale


def kernel(
    student, teacher, out,
    quarter_s, quarter_t, full_s, full_t, far, cols, extra, own, total, other,
    rs_send, rs_recv, gathered, acc, load_sem, send_sem, recv_sem,
):
    rows, width = student.shape
    margin = 0.75 / math.sqrt(width)
    weight = 64.0 * width / math.sqrt(rows * lax.axis_size("seq"))

    seq, pair = lax.axis_index("seq"), lax.axis_index("pair")
    core, y, z_hi = seq % 2, (seq // 2) % 4, seq // 8
    z_lo, x = pair // 4, pair % 4
    z = z_hi * 2 + z_lo
    side = 2 * z_lo - 1

    def device(x=x, y=y, z=z, core=core):
        return ((z // 2 * 4 + y) * 2 + core, (z % 2) * 4 + x)

    up, down = device(y=(y + 1) % 4), device(y=(y + 3) % 4)
    near_z = device(z=(z + side + 8) % 8)
    after_z, before_z = device(z=(z - 2 * side + 8) % 8), device(z=(z + 2 * side + 8) % 8)
    sibling = device(core=1 - core)
    cube = (device(x=x + 1 - 2 * (x % 2)), device(x=3 - x), device(z=z + 1 - 2 * z_lo))
    bits = (((x + 1) // 2) % 2, x // 2, z_lo)

    def copy(name, src, dst, target):
        i = INDEX[name]
        return pltpu.make_async_remote_copy(
            src_ref=src, dst_ref=dst, send_sem=send_sem.at[i], recv_sem=recv_sem.at[i],
            device_id=target, device_id_type=MESH,
        )

    started = {}

    def send(name, src, dst, target):
        started[name] = copy(name, src, dst, target)
        started[name].start()

    def arrived(*names):
        for name in names:
            started[name].wait_recv()

    first = pl.multiple_of(x * (2 * UNIT), 2 * UNIT)
    loads = [
        pltpu.make_async_copy(student.at[pl.ds(first, 2 * UNIT)], quarter_s, load_sem.at[0]),
        pltpu.make_async_copy(teacher.at[pl.ds(first, 2 * UNIT)], quarter_t, load_sem.at[1]),
        pltpu.make_async_copy(student, full_s, load_sem.at[2]),
        pltpu.make_async_copy(teacher, full_t, load_sem.at[3]),
    ]
    for load in loads:
        load.start()

    barrier = pltpu.get_barrier_semaphore()
    peers = (up, down, near_z, after_z, before_z, sibling) + cube
    for peer in peers:
        pl.semaphore_signal(barrier, inc=1, device_id=peer, device_id_type=MESH)

    def slot(i):
        return cols.at[pl.ds(i * UNIT, UNIT)]

    (A, A_DOWN, A_UP, V, V_DOWN, V_UP, W, A_FAR, V_FAR, Q_DOWN,
     W_DOWN, W_UP, Q_UP, Q_FAR, W_FAR, Q) = range(16)

    loads[0].wait()
    loads[1].wait()
    mine = pl.multiple_of(z_lo * UNIT, UNIT)
    theirs = pl.multiple_of((1 - z_lo) * UNIT, UNIT)
    far[:, :width] = normalize(quarter_s[pl.ds(theirs, UNIT)], width)[1].astype(jnp.bfloat16)
    far[:, width:] = normalize(quarter_t[pl.ds(theirs, UNIT)], width)[1].astype(jnp.bfloat16)
    cols[:UNIT, :width] = normalize(quarter_s[pl.ds(mine, UNIT)], width)[1].astype(jnp.bfloat16)
    cols[:UNIT, width:] = normalize(quarter_t[pl.ds(mine, UNIT)], width)[1].astype(jnp.bfloat16)
    pl.semaphore_wait(barrier, len(peers))
    send("v", far, slot(V), near_z)
    send("a+", slot(A), slot(A_DOWN), up)
    send("a-", slot(A), slot(A_UP), down)

    loads[2].wait()
    loads[3].wait()
    for half in range(2):

        @pl.loop(0, TILE // UNIT)
        def _(i):
            at = pl.ds(pl.multiple_of(half * TILE + i * UNIT, UNIT), UNIT)
            own[0, at, :width] = normalize(full_s[at], width)[1].astype(jnp.bfloat16)
            own[0, at, width:] = -(normalize(full_t[at], width)[1].astype(jnp.bfloat16))
            total[0, at] = jnp.zeros((UNIT, width), jnp.float32)
            total[1, at] = jnp.zeros((UNIT, width), jnp.float32)

        at = pl.ds(half * TILE, TILE)
        send(f"k{half}", own.at[0, at], own.at[1, at], sibling)

    def relate(partner, start, block, tile):
        at, tokens = pl.ds(tile * TILE, TILE), pl.ds(start, GROUP)
        delta = lax.dot_general(
            own[block, at, :], partner[tokens, :], (((1,), (1,)), ((), ())),
            preferred_element_type=jnp.float32,
        )
        shrink = jnp.maximum(delta - margin, 0.0) + jnp.minimum(delta + margin, 0.0)
        relation = (weight * shrink).astype(jnp.bfloat16)
        for first, size in PARTS:
            total[block, at, pl.ds(first, size)] += jnp.dot(
                relation, partner[tokens, pl.ds(first, size)], preferred_element_type=jnp.float32
            )

    def relate_all(group):
        @pl.loop(0, 2)
        def _(block):
            for tile in range(rows // TILE):
                relate(cols, group * GROUP, block, tile)

    def relate_own(partner, start):
        for tile in range(rows // TILE):
            relate(partner, start, 0, tile)

    def share(name, start, size):
        send(name, cols.at[pl.ds(4 * GROUP + start, size)], extra.at[pl.ds(start, size)], sibling)

    arrived("v")
    send("v+", slot(V), slot(V_DOWN), up)
    send("v-", slot(V), slot(V_UP), down)
    send("w", slot(V), slot(W), after_z)
    arrived("a+", "a-")
    send("af", slot(A_DOWN), slot(A_FAR), up)
    send("qd", slot(A_DOWN), slot(Q_DOWN), near_z)
    send("qu", slot(A_UP), slot(Q_UP), near_z)
    send("q", slot(A), slot(Q), near_z)
    arrived("k0", "k1")
    relate_all(0)
    arrived("v+", "v-")
    send("vf", slot(V_UP), slot(V_FAR), down)
    arrived("w")
    send("w+", slot(W), slot(W_DOWN), up)
    send("w-", slot(W), slot(W_UP), down)
    relate_all(1)
    arrived("qd")
    send("qf", slot(Q_DOWN), slot(Q_FAR), up)
    arrived("af", "vf")
    relate_all(2)
    arrived("w-")
    send("wf", slot(W_UP), slot(W_FAR), down)
    arrived("w+", "qu")
    share("e0", 0, 16)
    relate_all(3)
    send("x", total.at[1], other, sibling)
    for i, name in enumerate(("qf", "wf", "q")):
        arrived(name)
        share(f"e{i + 1}", 16 + i * UNIT, UNIT)
    relate_own(cols, 4 * GROUP)
    arrived("x", "e0", "e1", "e2", "e3")
    relate_own(extra, 0)

    def chunk(wave, order, *place):
        strides = (4, 2, 1)
        index = sum(strides[d] * i for d, i in zip(order, place))
        skip, size = WAVES[wave]
        return pl.ds(pl.multiple_of(index * UNIT + skip, 16), size)

    def each():
        for wave in range(2):
            for part, (start, size) in enumerate(PARTS):
                order = ORDERS[part]
                yield wave, part, order, [bits[d] for d in order], pl.ds(start, size), pl.ds(*WAVES[wave])

    def reduce(step, wave, part, order, first, count):
        at = (pl.ds(first, count), pl.ds(*WAVES[wave]))
        send(f"r{part}{step}{wave}", rs_send[part].at[at], rs_recv[part].at[at], cube[order[step]])

    for wave, part, order, b, at, sub in each():
        for i in range(4):
            rows_at = chunk(wave, order, 1 - b[0], i // 2, i % 2)
            rs_send[part][i, sub] = (total[0, rows_at, at] + other[rows_at, at]).astype(jnp.bfloat16)
        reduce(0, wave, part, order, 0, 4)
    for wave, part, order, b, at, sub in each():
        arrived(f"r{part}0{wave}")
        for i in range(2):
            rows_at = chunk(wave, order, b[0], 1 - b[1], i)
            got = rs_recv[part][2 * (1 - b[1]) + i, sub].astype(jnp.float32)
            rs_send[part][4 + i, sub] = (
                total[0, rows_at, at] + other[rows_at, at] + got
            ).astype(jnp.bfloat16)
        reduce(1, wave, part, order, 4, 2)
    for wave, part, order, b, at, sub in each():
        arrived(f"r{part}1{wave}")
        for i, place in enumerate((1 - b[2], b[2])):
            rows_at = chunk(wave, order, b[0], b[1], place)
            value = (
                total[0, rows_at, at] + other[rows_at, at]
                + rs_recv[part][2 * b[1] + place, sub].astype(jnp.float32)
                + rs_recv[part][4 + place, sub].astype(jnp.float32)
            )
            if i == 0:
                rs_send[part][6, sub] = value.astype(jnp.bfloat16)
                reduce(2, wave, part, order, 6, 1)
            else:
                acc[sub, at] = value

    def spread(step, wave, part, order, *place):
        there = gathered[part].at[place + (slice(None),) * step + (pl.ds(*WAVES[wave]),)]
        send(f"g{part}{step}{wave}", there, there, cube[order[2 - step]])

    for wave in range(2):
        sub = pl.ds(*WAVES[wave])
        for part, (start, size) in enumerate(PARTS):
            arrived(f"r{part}2{wave}")
            acc[sub, start:start + size] += rs_recv[part][6, sub].astype(jnp.float32)
        scale, unit = normalize(full_s[chunk(wave, (0, 1, 2), *bits)], width)
        unit_grad = acc[sub]
        dotted = jnp.sum(unit * unit_grad, axis=1, keepdims=True)
        grad = (scale * (unit_grad - unit * dotted)).astype(jnp.bfloat16)
        for part, (start, size) in enumerate(PARTS):
            order = ORDERS[part]
            b = [bits[d] for d in order]
            gathered[part][b[0], b[1], b[2], sub] = grad[:, start:start + size]
            spread(0, wave, part, order, *b)
    for wave, part, order, b, at, sub in each():
        arrived(f"g{part}0{wave}")
        spread(1, wave, part, order, b[0], b[1])
    for wave, part, order, b, at, sub in each():
        arrived(f"g{part}1{wave}")
        spread(2, wave, part, order, b[0])
    for wave, part, order, b, at, sub in each():
        arrived(f"g{part}2{wave}")
        for i in range(8):
            place = (i // 4, i // 2 % 2, i % 2)
            out[chunk(wave, (0, 1, 2), *place), at] = gathered[part][
                tuple(place[d] for d in order) + (sub,)
            ]
    for name in NAMES:
        started[name].wait_send()


def local(student, teacher):
    rows, width = student.shape
    bf16, f32 = jnp.bfloat16, jnp.float32

    def body(student, teacher, out, *scratch):
        plain, parts = scratch[:10], scratch[10:19]
        kernel(student, teacher, out, *plain, parts[0:3], parts[3:6], parts[6:9], *scratch[19:])

    grad = pl.pallas_call(
        body,
        out_shape=jax.ShapeDtypeStruct((rows, width), bf16),
        in_specs=[pl.BlockSpec(memory_space=pl.ANY)] * 2,
        out_specs=pl.BlockSpec(memory_space=pltpu.VMEM),
        scratch_shapes=[
            pltpu.VMEM((2 * UNIT, width), f32),
            pltpu.VMEM((2 * UNIT, width), f32),
            pltpu.VMEM((rows, width), f32),
            pltpu.VMEM((rows, width), f32),
            pltpu.VMEM((UNIT, 2 * width), bf16),
            pltpu.VMEM((2 * rows, 2 * width), bf16),
            pltpu.VMEM((GROUP, 2 * width), bf16),
            pltpu.VMEM((2, rows, 2 * width), bf16),
            pltpu.VMEM((2, rows, width), f32),
            pltpu.VMEM((rows, width), f32),
        ]
        + [pltpu.VMEM((7, UNIT, size), bf16) for _, size in PARTS] * 2
        + [pltpu.VMEM((2, 2, 2, UNIT, size), bf16) for _, size in PARTS]
        + [
            pltpu.VMEM((UNIT, width), f32),
            pltpu.SemaphoreType.DMA((4,)),
            pltpu.SemaphoreType.DMA((len(NAMES),)),
            pltpu.SemaphoreType.DMA((len(NAMES),)),
        ],
        compiler_params=pltpu.CompilerParams(
            collective_id=0, has_side_effects=True, vmem_limit_bytes=56 << 20
        ),
        name="relation_grad",
    )(student, teacher)
    return grad.astype(f32)


def solution(mesh):
    placed = (P("seq", None), P("seq", None))
    return jax.shard_map(
        local, mesh=mesh, in_specs=placed, out_specs=P("seq", None), check_vma=False
    )
```

time: 127 us -> 106 us (0.83)
  Pallas kernels: 123 us -> 101 us
    pallas_call x1, Pallas kernels: 123 us -> 101 us  [local(): pl.pallas_call(body, out_shape=jax.ShapeDtypeStruct((rows, width), bf16),...]
where the time goes in v2:
time: 106 us; the launch traced here: 104 us
  Pallas kernels  101 us (95%)
  other arithmetic  3.56 us (3%)
    pallas_call x1, Pallas kernels, local(): pl.pallas_call(body, out_shape=jax.ShapeDtypeStruct((rows, width), bf16),...  101 us
    convert_element_type x1, other arithmetic, local(): return grad.astype(f32)  3.56 us

profile of v2, /device:TPU:2, one launch (start us, length us, event | category | flops | bytes accessed | tf_op | source)
XLA Modules:
  0.0 104.5 jit_solution(15856030194701486579)
XLA Ops:
  0.0 100.9 %relation_grad.1 = bf16[640,1408]{1,0:T(8,128)(2,1)} custom-call(f32[640,1408]{1,0:T(8,128)} %student.1, f32[640,1408]{1,0:T(8,128)} %teacher.1), custom_call_target="tpu_custom_call" | custom-call | tf_op jit(solution)/shard_map/relation_grad/pallas_call | solution.py:273
  100.9 3.6 %convert_element_type.3 = f32[640,1408]{1,0:T(8,128)} convert(bf16[640,1408]{1,0:T(8,128)(2,1)} %relation_grad.1) | non-fusion elementwise | flops 901120 | bytes 5406720 | tf_op jit(solution)/shard_map/convert_element_type | solution.py:303

commit v3 on v2

v3 whole, which is shorter than its diff:
```python
import functools
import math

import jax
import jax.numpy as jnp
from jax import lax
from jax.experimental import pallas as pl
from jax.experimental.pallas import tpu as pltpu
from jax.sharding import PartitionSpec as P

MESH = pl.DeviceIdType.MESH
UNIT = 80
GROUP = 256
TILE = 320
HALVES = ((0, 48), (48, 32))
WAVES = ((0, 32), (32, 32), (64, 16))
APART = 2
PARTS = ((0, 512), (512, 512), (1024, 384))
ORDERS = ((0, 1, 2), (1, 2, 0), (2, 0, 1))

NAMES = (
    [f"{item}{half}" for half in range(2) for item in (
        "v", "q", "w", "qd", "qu", "qf", "a+", "a-", "af", "v+", "v-", "vf", "w+", "w-", "wf",
        "eqf", "ewf", "eq", "k", "x")]
    + ["e"]
    + [f"{kind}{part}{step}{wave}" for kind in "rg"
       for part in range(3) for step in range(3) for wave in range(len(WAVES))]
)
INDEX = {name: i for i, name in enumerate(NAMES)}


def normalize(values, width):
    scale = lax.rsqrt(jnp.sum(values * values, axis=1, keepdims=True) + width * 1e-06)
    return scale, values * scale


def kernel(
    student, teacher, out,
    quarter_s, quarter_t, full_s, full_t, far, cols, extra, own, total, other,
    rs_send, rs_recv, gathered, acc, load_sem, send_sem, recv_sem,
):
    rows, width = student.shape
    margin = 0.75 / math.sqrt(width)
    weight = 64.0 * width / math.sqrt(rows * lax.axis_size("seq"))

    seq, pair = lax.axis_index("seq"), lax.axis_index("pair")
    core, y, z_hi = seq % 2, (seq // 2) % 4, seq // 8
    z_lo, x = pair // 4, pair % 4
    z = z_hi * 2 + z_lo
    side = 2 * z_lo - 1

    def device(x=x, y=y, z=z, core=core):
        return ((z // 2 * 4 + y) * 2 + core, (z % 2) * 4 + x)

    up, down = device(y=(y + 1) % 4), device(y=(y + 3) % 4)
    near_z = device(z=(z + side + 8) % 8)
    after_z, before_z = device(z=(z - 2 * side + 8) % 8), device(z=(z + 2 * side + 8) % 8)
    sibling = device(core=1 - core)
    cube = (device(x=x + 1 - 2 * (x % 2)), device(x=3 - x), device(z=z + 1 - 2 * z_lo))
    bits = (((x + 1) // 2) % 2, x // 2, z_lo)

    def copy(name, src, dst, target):
        i = INDEX[name]
        return pltpu.make_async_remote_copy(
            src_ref=src, dst_ref=dst, send_sem=send_sem.at[i], recv_sem=recv_sem.at[i],
            device_id=target, device_id_type=MESH,
        )

    started = {}

    def send(name, src, dst, target):
        started[name] = copy(name, src, dst, target)
        started[name].start()

    def arrived(*names):
        for name in names:
            started[name].wait_recv()

    barrier = pltpu.get_barrier_semaphore()
    peers = (up, down, near_z, after_z, before_z, sibling) + cube
    for peer in peers:
        pl.semaphore_signal(barrier, inc=1, device_id=peer, device_id_type=MESH)

    first = pl.multiple_of(x * (2 * UNIT), 2 * UNIT)
    loads = [
        pltpu.make_async_copy(student.at[pl.ds(first, 2 * UNIT)], quarter_s, load_sem.at[0]),
        pltpu.make_async_copy(teacher.at[pl.ds(first, 2 * UNIT)], quarter_t, load_sem.at[1]),
        pltpu.make_async_copy(student, full_s, load_sem.at[2]),
        pltpu.make_async_copy(teacher, full_t, load_sem.at[3]),
    ]
    loads[0].start()
    loads[1].start()

    (A, A_DOWN, A_UP, V, V_DOWN, V_UP, W, A_FAR, V_FAR, Q_DOWN,
     W_DOWN, W_UP, Q_UP, Q_FAR, W_FAR, Q) = range(16)

    def move(name, half, src, dst, target):
        skip, size = HALVES[half]
        send(f"{name}{half}", cols.at[pl.ds(src * UNIT + skip, size)],
             cols.at[pl.ds(dst * UNIT + skip, size)], target)

    loads[0].wait()
    loads[1].wait()
    loads[2].start()
    loads[3].start()
    for half, (skip, size) in enumerate(HALVES):
        here, mine, theirs = (
            pl.ds(pl.multiple_of(at + skip, 16), size) for at in (0, z_lo * UNIT, (1 - z_lo) * UNIT)
        )
        far[here, :width] = normalize(quarter_s[theirs], width)[1].astype(jnp.bfloat16)
        far[here, width:] = normalize(quarter_t[theirs], width)[1].astype(jnp.bfloat16)
        cols[here, :width] = normalize(quarter_s[mine], width)[1].astype(jnp.bfloat16)
        cols[here, width:] = normalize(quarter_t[mine], width)[1].astype(jnp.bfloat16)
        if half == 0:
            pl.semaphore_wait(barrier, len(peers))
        send(f"v{half}", far.at[here], cols.at[pl.ds(V * UNIT + skip, size)], near_z)
        move("a+", half, A, A_DOWN, up)
        move("a-", half, A, A_UP, down)

    loads[2].wait()
    loads[3].wait()
    for half in range(2):

        @pl.loop(0, TILE // UNIT)
        def _(i):
            at = pl.ds(pl.multiple_of(half * TILE + i * UNIT, UNIT), UNIT)
            own[0, at, :width] = normalize(full_s[at], width)[1].astype(jnp.bfloat16)
            own[0, at, width:] = -(normalize(full_t[at], width)[1].astype(jnp.bfloat16))
            total[0, at] = jnp.zeros((UNIT, width), jnp.float32)
            total[1, at] = jnp.zeros((UNIT, width), jnp.float32)

        at = pl.ds(half * TILE, TILE)
        send(f"k{half}", own.at[0, at], own.at[1, at], sibling)

    def relate(partner, start, block, tile):
        at, tokens = pl.ds(tile * TILE, TILE), pl.ds(start, GROUP)
        delta = lax.dot_general(
            own[block, at, :], partner[tokens, :], (((1,), (1,)), ((), ())),
            preferred_element_type=jnp.float32,
        )
        shrink = jnp.maximum(delta - margin, 0.0) + jnp.minimum(delta + margin, 0.0)
        relation = (weight * shrink).astype(jnp.bfloat16)
        for first, size in PARTS:
            total[block, at, pl.ds(first, size)] += jnp.dot(
                relation, partner[tokens, pl.ds(first, size)], preferred_element_type=jnp.float32
            )

    def relate_all(group):
        @pl.loop(0, 2)
        def _(block):
            for tile in range(rows // TILE):
                relate(cols, group * GROUP, block, tile)

    def relate_own(partner, start):
        for tile in range(rows // TILE):
            relate(partner, start, 0, tile)

    def share(name, start, size):
        send(name, cols.at[pl.ds(4 * GROUP + start, size)], extra.at[pl.ds(start, size)], sibling)

    for half in range(2):
        arrived(f"v{half}")
        move("v+", half, V, V_DOWN, up)
        move("v-", half, V, V_UP, down)
        move("w", half, V, W, after_z)
    for half in range(2):
        arrived(f"a+{half}", f"a-{half}")
        move("qd", half, A_DOWN, Q_DOWN, near_z)
        move("af", half, A_DOWN, A_FAR, up)
    for half in range(2):
        move("qu", half, A_UP, Q_UP, near_z)
    for half in range(2):
        move("q", half, A, Q, near_z)
    arrived("k0", "k1")
    relate_all(0)
    for half in range(2):
        arrived(f"v+{half}", f"v-{half}")
        move("vf", half, V_UP, V_FAR, down)
    for half in range(2):
        arrived(f"w{half}")
        move("w+", half, W, W_DOWN, up)
        move("w-", half, W, W_UP, down)
    relate_all(1)
    for half in range(2):
        arrived(f"qd{half}")
        move("qf", half, Q_DOWN, Q_FAR, up)
    arrived("af0", "vf0", "af1", "vf1")
    relate_all(2)
    for half in range(2):
        arrived(f"w-{half}", f"w+{half}")
        move("wf", half, W_UP, W_FAR, down)
    arrived("qu0", "qu1")
    share("e", 0, 16)
    for tile in range(2):
        at = pl.ds(tile * TILE, TILE)
        relate(cols, 3 * GROUP, 1, tile)
        send(f"x{tile}", total.at[1, at], other.at[at], sibling)
    relate_own(cols, 3 * GROUP)
    for half, (skip, size) in enumerate(HALVES):
        for i, name in enumerate(("qf", "wf", "q")):
            arrived(f"{name}{half}")
            share(f"e{name}{half}", 16 + i * UNIT + skip, size)
    relate_own(cols, 4 * GROUP)
    arrived("x0", "x1", "e", "eqf0", "ewf0", "eq0", "eqf1", "ewf1", "eq1")
    relate_own(extra, 0)

    def chunk(wave, order, *place):
        strides = (4, 2, 1)
        index = sum(strides[d] * i for d, i in zip(order, place))
        skip, size = WAVES[wave]
        return pl.ds(pl.multiple_of(index * UNIT + skip, 16), size)

    def parts(wave):
        for part, (start, size) in enumerate(PARTS):
            order = ORDERS[(part + wave) % 3]
            yield part, order, [bits[d] for d in order], pl.ds(start, size)

    def reduce(step, wave, part, order, first, count):
        at = (pl.ds(first, count), pl.ds(*WAVES[wave]))
        send(f"r{part}{step}{wave}", rs_send[part].at[at], rs_recv[part].at[at], cube[order[step]])

    def spread(step, wave, part, order, *place):
        there = gathered[part].at[place + (slice(None),) * step + (pl.ds(*WAVES[wave]),)]
        send(f"g{part}{step}{wave}", there, there, cube[order[2 - step]])

    def halve_first(wave):
        sub = pl.ds(*WAVES[wave])
        for part, order, b, at in parts(wave):
            for i in range(4):
                rows_at = chunk(wave, order, 1 - b[0], i // 2, i % 2)
                rs_send[part][i, sub] = (total[0, rows_at, at] + other[rows_at, at]).astype(jnp.bfloat16)
            reduce(0, wave, part, order, 0, 4)

    def halve_second(wave):
        sub = pl.ds(*WAVES[wave])
        for part, order, b, at in parts(wave):
            arrived(f"r{part}0{wave}")
            for i in range(2):
                rows_at = chunk(wave, order, b[0], 1 - b[1], i)
                got = rs_recv[part][2 * (1 - b[1]) + i, sub].astype(jnp.float32)
                rs_send[part][4 + i, sub] = (
                    total[0, rows_at, at] + other[rows_at, at] + got
                ).astype(jnp.bfloat16)
            reduce(1, wave, part, order, 4, 2)

    def halve_third(wave):
        sub = pl.ds(*WAVES[wave])
        for part, order, b, at in parts(wave):
            arrived(f"r{part}1{wave}")
            for i, place in enumerate((1 - b[2], b[2])):
                rows_at = chunk(wave, order, b[0], b[1], place)
                value = (
                    total[0, rows_at, at] + other[rows_at, at]
                    + rs_recv[part][2 * b[1] + place, sub].astype(jnp.float32)
                    + rs_recv[part][4 + place, sub].astype(jnp.float32)
                )
                if i == 0:
                    rs_send[part][6, sub] = value.astype(jnp.bfloat16)
                    reduce(2, wave, part, order, 6, 1)
                else:
                    acc[sub, at] = value

    def finish(wave):
        sub = pl.ds(*WAVES[wave])
        for part, order, b, at in parts(wave):
            arrived(f"r{part}2{wave}")
            acc[sub, at] += rs_recv[part][6, sub].astype(jnp.float32)
        scale, unit = normalize(full_s[chunk(wave, (0, 1, 2), *bits)], width)
        unit_grad = acc[sub]
        dotted = jnp.sum(unit * unit_grad, axis=1, keepdims=True)
        grad = (scale * (unit_grad - unit * dotted)).astype(jnp.bfloat16)
        for part, order, b, at in parts(wave):
            start, size = PARTS[part]
            gathered[part][b[0], b[1], b[2], sub] = grad[:, start:start + size]
            spread(0, wave, part, order, *b)

    def double_second(wave):
        for part, order, b, at in parts(wave):
            arrived(f"g{part}0{wave}")
            spread(1, wave, part, order, b[0], b[1])

    def double_third(wave):
        for part, order, b, at in parts(wave):
            arrived(f"g{part}1{wave}")
            spread(2, wave, part, order, b[0])

    def emit(wave):
        sub = pl.ds(*WAVES[wave])
        for part, order, b, at in parts(wave):
            arrived(f"g{part}2{wave}")
            for i in range(8):
                place = (i // 4, i // 2 % 2, i % 2)
                out[chunk(wave, (0, 1, 2), *place), at] = gathered[part][
                    tuple(place[d] for d in order) + (sub,)
                ]

    stages = (halve_first, halve_second, halve_third, finish, double_second, double_third, emit)
    steps = [(wave + APART * i, i, wave) for i in range(len(stages)) for wave in range(len(WAVES))]
    for _, i, wave in sorted(steps):
        stages[i](wave)
    for name in NAMES:
        started[name].wait_send()


def local(student, teacher):
    rows, width = student.shape
    bf16, f32 = jnp.bfloat16, jnp.float32

    def body(student, teacher, out, *scratch):
        plain, parts = scratch[:10], scratch[10:19]
        kernel(student, teacher, out, *plain, parts[0:3], parts[3:6], parts[6:9], *scratch[19:])

    grad = pl.pallas_call(
        body,
        out_shape=pltpu.VMEM((rows, width), bf16),
        in_specs=[pl.BlockSpec(memory_space=pl.ANY)] * 2,
        out_specs=pl.BlockSpec(memory_space=pltpu.VMEM),
        scratch_shapes=[
            pltpu.VMEM((2 * UNIT, width), f32),
            pltpu.VMEM((2 * UNIT, width), f32),
            pltpu.VMEM((rows, width), f32),
            pltpu.VMEM((rows, width), f32),
            pltpu.VMEM((UNIT, 2 * width), bf16),
            pltpu.VMEM((2 * rows, 2 * width), bf16),
            pltpu.VMEM((GROUP, 2 * width), bf16),
            pltpu.VMEM((2, rows, 2 * width), bf16),
            pltpu.VMEM((2, rows, width), f32),
            pltpu.VMEM((rows, width), f32),
        ]
        + [pltpu.VMEM((7, UNIT, size), bf16) for _, size in PARTS] * 2
        + [pltpu.VMEM((2, 2, 2, UNIT, size), bf16) for _, size in PARTS]
        + [
            pltpu.VMEM((UNIT, width), f32),
            pltpu.SemaphoreType.DMA((4,)),
            pltpu.SemaphoreType.DMA((len(NAMES),)),
            pltpu.SemaphoreType.DMA((len(NAMES),)),
        ],
        compiler_params=pltpu.CompilerParams(
            collective_id=0, has_side_effects=True, vmem_limit_bytes=56 << 20
        ),
        name="relation_grad",
    )(student, teacher)
    return grad.astype(f32)


def solution(mesh):
    placed = (P("seq", None), P("seq", None))
    return jax.shard_map(
        local, mesh=mesh, in_specs=placed, out_specs=P("seq", None), check_vma=False
    )
```

time: 106 us -> 100 us (0.943); the launches traced: 104 us -> 100 us
  Pallas kernels: 101 us -> 98.1 us
  other arithmetic: 3.56 us -> 2.07 us
    pallas_call x1, Pallas kernels: 101 us -> 98.1 us  [local(): pl.pallas_call(body, out_shape=pltpu.VMEM((rows, width), bf16), in_specs=...]
    convert_element_type x1, other arithmetic: 3.56 us -> 2.07 us  [local(): return grad.astype(f32)]
where the time goes in v3:
time: 100 us
  Pallas kernels  98.1 us (98%)
  other arithmetic  2.07 us (2%)
    pallas_call x1, Pallas kernels, local(): pl.pallas_call(body, out_shape=pltpu.VMEM((rows, width), bf16), in_specs=...  98.1 us
    convert_element_type x1, other arithmetic, local(): return grad.astype(f32)  2.07 us

profile of v3, /device:TPU:2, one launch (start us, length us, event | category | flops | bytes accessed | tf_op | source)
XLA Modules:
  0.0 100.2 jit_solution(5912383405502861666)
XLA Ops:
  0.0 98.1 %relation_grad.1 = bf16[640,1408]{1,0:T(8,128)(2,1)S(1)} custom-call(f32[640,1408]{1,0:T(8,128)} %student.1, f32[640,1408]{1,0:T(8,128)} %teacher.1), custom_call_target="tpu_custom_call" | custom-call | tf_op jit(solution)/shard_map/relation_grad/pallas_call | solution.py:313
  98.1 2.1 %convert_element_type.3 = f32[640,1408]{1,0:T(8,128)} convert(bf16[640,1408]{1,0:T(8,128)(2,1)S(1)} %relation_grad.1) | non-fusion elementwise | flops 901120 | bytes 5406720 | tf_op jit(solution)/shard_map/convert_element_type | solution.py:343

commit v4 on v3

--- a/solution.py
+++ b/solution.py
@@ -12,17 +12,14 @@
 UNIT = 80
 GROUP = 256
 TILE = 320
-HALVES = ((0, 48), (48, 32))
 WAVES = ((0, 32), (32, 32), (64, 16))
 APART = 2
 PARTS = ((0, 512), (512, 512), (1024, 384))
 ORDERS = ((0, 1, 2), (1, 2, 0), (2, 0, 1))
 
 NAMES = (
-    [f"{item}{half}" for half in range(2) for item in (
-        "v", "q", "w", "qd", "qu", "qf", "a+", "a-", "af", "v+", "v-", "vf", "w+", "w-", "wf",
-        "eqf", "ewf", "eq", "k", "x")]
-    + ["e"]
+    ["v", "q", "w", "qd", "qu", "qf", "a+", "a-", "af", "v+", "v-", "vf", "w+", "w-", "wf"]
+    + ["e", "eqf", "ewf", "eq", "k0", "k1", "x0", "x1"]
     + [f"{kind}{part}{step}{wave}" for kind in "rg"
        for part in range(3) for step in range(3) for wave in range(len(WAVES))]
 )
@@ -37,7 +34,7 @@
 def kernel(
     student, teacher, out,
     quarter_s, quarter_t, full_s, full_t, far, cols, extra, own, total, other,
-    rs_send, rs_recv, gathered, acc, load_sem, send_sem, recv_sem,
+    rs_send, rs_recv, gathered, acc, own_unit, own_scale, load_sem, send_sem, recv_sem,
 ):
     rows, width = student.shape
     margin = 0.75 / math.sqrt(width)
@@ -94,28 +91,27 @@
     (A, A_DOWN, A_UP, V, V_DOWN, V_UP, W, A_FAR, V_FAR, Q_DOWN,
      W_DOWN, W_UP, Q_UP, Q_FAR, W_FAR, Q) = range(16)
 
-    def move(name, half, src, dst, target):
-        skip, size = HALVES[half]
-        send(f"{name}{half}", cols.at[pl.ds(src * UNIT + skip, size)],
-             cols.at[pl.ds(dst * UNIT + skip, size)], target)
-
     loads[0].wait()
     loads[1].wait()
     loads[2].start()
     loads[3].start()
-    for half, (skip, size) in enumerate(HALVES):
-        here, mine, theirs = (
-            pl.ds(pl.multiple_of(at + skip, 16), size) for at in (0, z_lo * UNIT, (1 - z_lo) * UNIT)
-        )
-        far[here, :width] = normalize(quarter_s[theirs], width)[1].astype(jnp.bfloat16)
-        far[here, width:] = normalize(quarter_t[theirs], width)[1].astype(jnp.bfloat16)
-        cols[here, :width] = normalize(quarter_s[mine], width)[1].astype(jnp.bfloat16)
-        cols[here, width:] = normalize(quarter_t[mine], width)[1].astype(jnp.bfloat16)
-        if half == 0:
-            pl.semaphore_wait(barrier, len(peers))
-        send(f"v{half}", far.at[here], cols.at[pl.ds(V * UNIT + skip, size)], near_z)
-        move("a+", half, A, A_DOWN, up)
-        move("a-", half, A, A_UP, down)
+    def quarter(dst, start):
+        at = pl.ds(pl.multiple_of(start * UNIT, UNIT), UNIT)
+        dst[:, :width] = normalize(quarter_s[at], width)[1].astype(jnp.bfloat16)
+        dst[:, width:] = normalize(quarter_t[at], width)[1].astype(jnp.bfloat16)
+
+    def slot(i):
+        return cols.at[pl.ds(i * UNIT, UNIT)]
+
+    def move(name, src, dst, target):
+        send(name, slot(src), slot(dst), target)
+
+    quarter(far, 1 - z_lo)
+    pl.semaphore_wait(barrier, len(peers))
+    send("v", far, slot(V), near_z)
+    quarter(slot(A), z_lo)
+    move("a+", A, A_DOWN, up)
+    move("a-", A, A_UP, down)
 
     loads[2].wait()
     loads[3].wait()
@@ -158,50 +154,45 @@
     def share(name, start, size):
         send(name, cols.at[pl.ds(4 * GROUP + start, size)], extra.at[pl.ds(start, size)], sibling)
 
-    for half in range(2):
-        arrived(f"v{half}")
-        move("v+", half, V, V_DOWN, up)
-        move("v-", half, V, V_UP, down)
-        move("w", half, V, W, after_z)
-    for half in range(2):
-        arrived(f"a+{half}", f"a-{half}")
-        move("qd", half, A_DOWN, Q_DOWN, near_z)
-        move("af", half, A_DOWN, A_FAR, up)
-    for half in range(2):
-        move("qu", half, A_UP, Q_UP, near_z)
-    for half in range(2):
-        move("q", half, A, Q, near_z)
+    arrived("v")
+    move("v+", V, V_DOWN, up)
+    move("v-", V, V_UP, down)
+    move("w", V, W, after_z)
+    arrived("a+", "a-")
+    move("qd", A_DOWN, Q_DOWN, near_z)
+    move("af", A_DOWN, A_FAR, up)
+    move("qu", A_UP, Q_UP, near_z)
+    move("q", A, Q, near_z)
     arrived("k0", "k1")
     relate_all(0)
-    for half in range(2):
-        arrived(f"v+{half}", f"v-{half}")
-        move("vf", half, V_UP, V_FAR, down)
-    for half in range(2):
-        arrived(f"w{half}")
-        move("w+", half, W, W_DOWN, up)
-        move("w-", half, W, W_UP, down)
+    arrived("v+", "v-")
+    move("vf", V_UP, V_FAR, down)
+    arrived("w")
+    move("w+", W, W_DOWN, up)
+    move("w-", W, W_UP, down)
     relate_all(1)
-    for half in range(2):
-        arrived(f"qd{half}")
-        move("qf", half, Q_DOWN, Q_FAR, up)
-    arrived("af0", "vf0", "af1", "vf1")
+    arrived("qd")
+    move("qf", Q_DOWN, Q_FAR, up)
+    arrived("af", "vf")
     relate_all(2)
-    for half in range(2):
-        arrived(f"w-{half}", f"w+{half}")
-        move("wf", half, W_UP, W_FAR, down)
-    arrived("qu0", "qu1")
+    arrived("w-")
+    move("wf", W_UP, W_FAR, down)
+    arrived("w+", "qu")
     share("e", 0, 16)
     for tile in range(2):
         at = pl.ds(tile * TILE, TILE)
         relate(cols, 3 * GROUP, 1, tile)
         send(f"x{tile}", total.at[1, at], other.at[at], sibling)
     relate_own(cols, 3 * GROUP)
-    for half, (skip, size) in enumerate(HALVES):
-        for i, name in enumerate(("qf", "wf", "q")):
-            arrived(f"{name}{half}")
-            share(f"e{name}{half}", 16 + i * UNIT + skip, size)
+    place = pl.multiple_of(((bits[0] * 2 + bits[1]) * 2 + bits[2]) * UNIT, UNIT)
+    scale, unit = normalize(full_s[pl.ds(place, UNIT)], width)
+    own_unit[...] = unit
+    own_scale[...] = jnp.broadcast_to(scale, own_scale.shape)
+    for i, name in enumerate(("qf", "wf", "q")):
+        arrived(name)
+        share(f"e{name}", 16 + i * UNIT, UNIT)
     relate_own(cols, 4 * GROUP)
-    arrived("x0", "x1", "e", "eqf0", "ewf0", "eq0", "eqf1", "ewf1", "eq1")
+    arrived("x0", "x1", "e", "eqf", "ewf", "eq")
     relate_own(extra, 0)
 
     def chunk(wave, order, *place):
@@ -265,7 +256,7 @@
         for part, order, b, at in parts(wave):
             arrived(f"r{part}2{wave}")
             acc[sub, at] += rs_recv[part][6, sub].astype(jnp.float32)
-        scale, unit = normalize(full_s[chunk(wave, (0, 1, 2), *bits)], width)
+        scale, unit = own_scale[sub, :1], own_unit[sub]
         unit_grad = acc[sub]
         dotted = jnp.sum(unit * unit_grad, axis=1, keepdims=True)
         grad = (scale * (unit_grad - unit * dotted)).astype(jnp.bfloat16)
@@ -292,7 +283,7 @@
                 place = (i // 4, i // 2 % 2, i % 2)
                 out[chunk(wave, (0, 1, 2), *place), at] = gathered[part][
                     tuple(place[d] for d in order) + (sub,)
-                ]
+                ].astype(jnp.float32)
 
     stages = (halve_first, halve_second, halve_third, finish, double_second, double_third, emit)
     steps = [(wave + APART * i, i, wave) for i in range(len(stages)) for wave in range(len(WAVES))]
@@ -312,7 +303,7 @@
 
     grad = pl.pallas_call(
         body,
-        out_shape=pltpu.VMEM((rows, width), bf16),
+        out_shape=pltpu.VMEM((rows, width), f32),
         in_specs=[pl.BlockSpec(memory_space=pl.ANY)] * 2,
         out_specs=pl.BlockSpec(memory_space=pltpu.VMEM),
         scratch_shapes=[
@@ -331,6 +322,8 @@
         + [pltpu.VMEM((2, 2, 2, UNIT, size), bf16) for _, size in PARTS]
         + [
             pltpu.VMEM((UNIT, width), f32),
+            pltpu.VMEM((UNIT, width), f32),
+            pltpu.VMEM((UNIT, 128), f32),
             pltpu.SemaphoreType.DMA((4,)),
             pltpu.SemaphoreType.DMA((len(NAMES),)),
             pltpu.SemaphoreType.DMA((len(NAMES),)),
@@ -340,7 +333,7 @@
         ),
         name="relation_grad",
     )(student, teacher)
-    return grad.astype(f32)
+    return grad
 
 
 def solution(mesh):

time: 100 us -> 99.2 us (level)
  other arithmetic: 2.07 us -> 0 us
  local copies, waits for them, and re-layouts: 0 us -> 1.82 us
  Pallas kernels: 98.1 us -> 96.6 us
    convert_element_type x1 -> x0, other arithmetic: 2.07 us -> none  [local(): return grad.astype(f32)]
    unnamed x0 -> x1, local copies, waits for them, and re-layouts: none -> 1.82 us
    pallas_call x1, Pallas kernels: 98.1 us -> 96.6 us  [local(): pl.pallas_call(body, out_shape=pltpu.VMEM((rows, width), f32), in_specs=[...]
where the time goes in v4:
time: 99.2 us; the launch traced here: 98.5 us
  Pallas kernels  96.6 us (97%)
  local copies, waits for them, and re-layouts  1.82 us (2%)
    pallas_call x1, Pallas kernels, local(): pl.pallas_call(body, out_shape=pltpu.VMEM((rows, width), f32), in_specs=[...  96.6 us

profile of v4, /device:TPU:2, one launch (start us, length us, event | category | flops | bytes accessed | tf_op | source)
XLA Modules:
  0.0 98.5 jit_solution(15087371098093504302)
XLA Ops:
  0.0 96.6 %relation_grad.1 = f32[640,1408]{1,0:T(8,128)S(1)} custom-call(f32[640,1408]{1,0:T(8,128)} %student.1, f32[640,1408]{1,0:T(8,128)} %teacher.1), custom_call_target="tpu_custom_call" | custom-call | tf_op jit(solution)/shard_map/relation_grad/pallas_call | solution.py:304
  96.6 1.8 %copy.4 = f32[640,1408]{1,0:T(8,128)} copy(f32[640,1408]{1,0:T(8,128)S(1)} %relation_grad.1) | data formatting | bytes 7208960

commit v5 on v4

--- a/solution.py
+++ b/solution.py
@@ -128,17 +128,17 @@
         at = pl.ds(half * TILE, TILE)
         send(f"k{half}", own.at[0, at], own.at[1, at], sibling)
 
-    def relate(partner, start, block, tile):
-        at, tokens = pl.ds(tile * TILE, TILE), pl.ds(start, GROUP)
+    def relate(partner, start, block, tile, size=TILE):
+        at, tokens = pl.ds(tile * size, size), pl.ds(start, GROUP)
         delta = lax.dot_general(
             own[block, at, :], partner[tokens, :], (((1,), (1,)), ((), ())),
             preferred_element_type=jnp.float32,
         )
         shrink = jnp.maximum(delta - margin, 0.0) + jnp.minimum(delta + margin, 0.0)
         relation = (weight * shrink).astype(jnp.bfloat16)
-        for first, size in PARTS:
-            total[block, at, pl.ds(first, size)] += jnp.dot(
-                relation, partner[tokens, pl.ds(first, size)], preferred_element_type=jnp.float32
+        for first, wide in PARTS:
+            total[block, at, pl.ds(first, wide)] += jnp.dot(
+                relation, partner[tokens, pl.ds(first, wide)], preferred_element_type=jnp.float32
             )
 
     def relate_all(group):
@@ -148,8 +148,7 @@
                 relate(cols, group * GROUP, block, tile)
 
     def relate_own(partner, start):
-        for tile in range(rows // TILE):
-            relate(partner, start, 0, tile)
+        relate(partner, start, 0, 0, rows)
 
     def share(name, start, size):
         send(name, cols.at[pl.ds(4 * GROUP + start, size)], extra.at[pl.ds(start, size)], sibling)
@@ -287,10 +286,21 @@
 
     stages = (halve_first, halve_second, halve_third, finish, double_second, double_third, emit)
     steps = [(wave + APART * i, i, wave) for i in range(len(stages)) for wave in range(len(WAVES))]
+    settled = set()
+
+    def settle(kinds):
+        for name in started:
+            if name[0] in kinds and name not in settled:
+                settled.add(name)
+                started[name].wait_send()
+
     for _, i, wave in sorted(steps):
+        if (i, wave) == (1, 0):
+            settle("vqawekx")
+        elif (i, wave) == (6, 0):
+            settle("r")
         stages[i](wave)
-    for name in NAMES:
-        started[name].wait_send()
+    settle("g")
 
 
 def local(student, teacher):

time: 99.2 us -> 98.8 us (level)
  no operation moved by 1% of the time
where the time goes in v5:
time: 98.8 us; the launch traced here: 98.1 us
  Pallas kernels  96.2 us (97%)
  local copies, waits for them, and re-layouts  1.82 us (2%)
    pallas_call x1, Pallas kernels, local(): pl.pallas_call(body, out_shape=pltpu.VMEM((rows, width), f32), in_specs=[...  96.2 us

profile of v5, /device:TPU:2, one launch (start us, length us, event | category | flops | bytes accessed | tf_op | source)
XLA Modules:
  0.0 98.1 jit_solution(2162914728587819643)
XLA Ops:
  0.0 96.2 %relation_grad.1 = f32[640,1408]{1,0:T(8,128)S(1)} custom-call(f32[640,1408]{1,0:T(8,128)} %student.1, f32[640,1408]{1,0:T(8,128)} %teacher.1), custom_call_target="tpu_custom_call" | custom-call | tf_op jit(solution)/shard_map/relation_grad/pallas_call | solution.py:314
  96.2 1.8 %copy.4 = f32[640,1408]{1,0:T(8,128)} copy(f32[640,1408]{1,0:T(8,128)S(1)} %relation_grad.1) | data formatting | bytes 7208960
